TPU v7x, 32 devices: a whole 2x2x4 slice. The times are simulated.
32 devices in a mesh: row: 4 (over y, core), col: 8 (over z, x).
Axes of the slice: x: 2, y: 2, z: 4, core: 2. Of those that a mesh axis runs over, the one named last changes fastest.
Arguments:
- transition: bfloat16 [32768, 32768], P('row', 'col'), may hold values from 1.5258789e-06 to 0.0024414062, as said below
- emission: bfloat16 [96, 32768], P(None, 'col'), may hold values from 0.0099487305 to 1
- token_ids: int32 [2, 192], replicated, may hold values from 0 to 95
- forward: bfloat16 [2, 192, 32768], P(None, 'col', 'row'), may hold values from 3.0517578e-06 to 0.0008239746, as said below
- backward_last: float32 [192, 32768], P('row', 'col'), may hold values from 0.1 to 10
Outputs:
- backward: float32 [2, 192, 32768], P(None, 'col', 'row')
- counts: float32 [32768, 1024], P('row', 'col')
Inputs may be any that keep to these rules, and one draw needn't show every extreme that they name: Positive transition weights. Positive forward weights.
All inputs are finite; a program needn't handle non-finite values.
Results may differ from a plain program's by a relative error of at most 0.00048.
Values may be sent and summed in bfloat16 or wider, within the bound.
A program may use at most 192 MiB of HBM per device.

v0:
```python
import jax
import jax.numpy as jnp
from jax import lax
from jax.sharding import PartitionSpec as P

H = 32768
N = 192
DW = 128
CHUNKS = 2


def reduce_scatter(partial, scale, col_count, col_index, local_seqs):
    half = col_count // 2
    width = partial.shape[1]
    scaled = (partial * scale).reshape(half, 2, local_seqs, width)
    side = col_index % 2
    away = lax.dynamic_index_in_dim(scaled, 1 - side, 1, keepdims=False).astype(jnp.float16)
    got = lax.ppermute(away, "col", [(c, c ^ 1) for c in range(col_count)])
    pair = lax.dynamic_index_in_dim(scaled, side, 1, keepdims=False) + got.astype(jnp.float32)
    here = col_index // 2
    total = lax.dynamic_index_in_dim(pair, here, 0, keepdims=False)
    packed = pair.astype(jnp.float16)
    for k in range(1, half):
        piece = lax.dynamic_index_in_dim(packed, (here + k) % half, 0, keepdims=False)
        got = lax.ppermute(piece, "col", [(c, (c + 2 * k) % col_count) for c in range(col_count)])
        total = total + got.astype(jnp.float32)
    return total


def on_device(transition, emission, token_ids, forward, backward_last):
    row_count = lax.axis_size("row")
    col_count = lax.axis_size("col")
    row_index = lax.axis_index("row")
    col_index = lax.axis_index("col")
    ratio = col_count // row_count
    local_seqs = forward.shape[1]
    row_seqs = backward_last.shape[0]
    block_src = transition.shape[0]
    block_dst = transition.shape[1]
    seq_total = local_seqs * col_count
    forward_all = [None, lax.all_gather(forward[1], "col", axis=0, tiled=True)]
    columns = lax.broadcasted_iota(jnp.int32, (row_seqs, emission.shape[0]), 1)
    window = transition[:, :DW]
    totals = jnp.zeros((block_src, DW), jnp.float32)
    outputs = [None, None]
    beta = backward_last
    scale = jnp.full((seq_total, 1), 64.0, jnp.float32)
    chunk = block_src // CHUNKS
    for step in (1, 0):
        tokens = lax.dynamic_slice_in_dim(token_ids[step], row_index * row_seqs, row_seqs, 0)
        onehot = (tokens[:, None] == columns).astype(jnp.bfloat16)
        emitted = jnp.dot(onehot, emission, preferred_element_type=jnp.float32)
        local_back = (emitted * beta).astype(jnp.bfloat16)
        weighted_back = lax.all_gather(local_back, "row", axis=0, tiled=True)
        pieces = []
        norm = jnp.zeros((seq_total,), jnp.float32)
        mass = jnp.zeros((seq_total,), jnp.float32)
        if step == 0:
            forward_all[0] = lax.all_gather(forward[0], "col", axis=0, tiled=True)
        for k in range(CHUNKS):
            rows = slice(k * chunk, (k + 1) * chunk)
            partial = lax.dot_general(
                weighted_back,
                transition[rows],
                (((1,), (1,)), ((), ())),
                preferred_element_type=jnp.float32,
            )
            norm = norm + jnp.sum(forward_all[step][:, rows].astype(jnp.float32) * partial, axis=1)
            mass = mass + jnp.sum(partial, axis=1)
            pieces.append(reduce_scatter(partial, scale, col_count, col_index, local_seqs))
        if step == 1:
            both = lax.psum(jnp.stack([norm, mass]), ("row", "col"))
            normal_all = both[0]
        else:
            normal_all = lax.psum(norm, ("row", "col"))
        normal_mine = lax.dynamic_slice_in_dim(normal_all, col_index * local_seqs, local_seqs, 0)
        scale_mine = lax.dynamic_slice_in_dim(scale, col_index * local_seqs, local_seqs, 0)
        mine = jnp.concatenate(pieces, axis=1) / (scale_mine * normal_mine[:, None])
        outputs[step] = mine
        if step == 1:
            halves = mine.reshape(local_seqs, ratio, block_dst)
            arrived = []
            for p in range(ratio):
                part = lax.dynamic_index_in_dim(halves, (col_index + p) % ratio, 1, keepdims=False)
                moves = []
                for r in range(row_count):
                    for c in range(col_count):
                        h = (c + p) % ratio
                        moves.append((r * col_count + c, c // ratio * col_count + r * ratio + h))
                arrived.append(lax.ppermute(part, ("row", "col"), moves))
            turned = jnp.stack([arrived[-i % ratio] for i in range(ratio)] * 2)
            start = (ratio - col_index % ratio) % ratio
            beta = lax.dynamic_slice_in_dim(turned, start, ratio, 0).reshape(row_seqs, block_dst)
            scale = (16777216.0 * both[0] / both[1])[:, None]
        scaled = (forward_all[step].astype(jnp.float32) / normal_all[:, None]).astype(jnp.bfloat16)
        totals = totals + lax.dot_general(
            scaled,
            weighted_back[:, :DW],
            (((0,), (0,)), ((), ())),
            preferred_element_type=jnp.float32,
        )
    counts = window.astype(jnp.float32) * totals * (H * H / N)
    return (jnp.stack(outputs), counts)


def solution(mesh):
    in_specs = (P("row", "col"), P(None, "col"), P(), P(None, "col", "row"), P("row", "col"))
    out_specs = (P(None, "col", "row"), P("row", "col"))
    return jax.shard_map(
        on_device, mesh=mesh, in_specs=in_specs, out_specs=out_specs, check_vma=False
    )
```

profile of v0, /device:TPU:0, one launch (start us, length us, event | category | flops | bytes accessed | tf_op | source)
XLA Modules:
  0.0 469.5 jit_solution(5049262565942433598)
XLA Ops:
  8.3 2.2 fusion.10
  10.6 2.0 fusion.50
  12.8 20.2 %all-gather.7.cloned.1.call-done = bf16[192,4096]{1,0:T(8,128)(2,1)} async-done(((bf16[48,4096]{1,0:T(8,128)(2,1)}), bf16[192,4096]{1,0:T(8,128)(2,1)}) %all-gather.7.cloned.1.call-update) | async-done | bytes 1572880 | tf_op jit(solution)/shard_map/all_gather | solution.py:54
  33.1 21.2 %fusion.6 = f32[192,4096]{1,0:T(8,128)} fusion(bf16[192,4096]{1,0:T(8,128)(2,1)} %all-gather.7.cloned.1.call-done, bf16[8192,4096]{1,0:T(8,128)(2,1)} %param.5), kind=kOutput, calls=%fused_computation.6 | convolution fusion | flops 6442450944 | bytes 38273024 | tf_op jit(solution)/shard_map/dot_general | solution.py:62
  54.3 42.0 %all-gather.11.cloned.1.call-done = bf16[1,192,8192]{2,1,0:T(8,128)(2,1)} async-done(((bf16[1,24,8192]{2,1,0:T(8,128)(2,1)}), bf16[1,192,8192]{2,1,0:T(8,128)(2,1)}) %all-gather.11.cloned.1.call-update) | async-done | bytes 3145744 | tf_op jit(solution)/shard_map/all_gather | solution.py:41
  96.3 20.1 %multiply_reduce_fusion.2 = (f32[192]{0:T(256)S(1)}, f32[192]{0:T(256)S(1)}, f32[192]{0:T(256)S(1)}, f32[192]{0:T(256)S(1)}, f32[192,4096]{1,0:T(8,128)}, /*index=5*/f32[192,4096]{1,0:T(8,128)}) fusion(bf16[192,8192]{1,0:T(8,128)(2,1)} %bitcast.147, f32[192,4096]{1,0:T(8,128)} %fusion.6, bf16[192,4096]{1,0:T(8,128)(2,1)S(1)} %copy-done.6, ...), kind=kOutput, calls=%fused_computation.18 | convolution fusion | flops 6450315264 | bytes 47713280 | tf_op jit(solution)/shard_map/dot_general | solution.py:62
  116.4 2.4 fusion.14
  120.9 1.5 collective-permute-start
  122.4 65.4 %psum.14 = f32[2,192]{1,0:T(2,128)S(1)} all-reduce(f32[2,192]{1,0:T(2,128)S(1)} %pad_maximum_fusion.1), channel_id=1, replica_groups=mesh['row'=4,'col'=8] {'row','col'}, use_global_device_ids=true, to_apply=%region_4.5 | all-reduce | flops 384 | bytes 3072 | tf_op jit(solution)/shard_map/psum | solution.py:72
  188.0 1.8 fusion.49
  190.8 2.9 collective-permute-start.7
  194.8 3.3 collective-permute-start.3
  198.0 1.5 collective-permute-done.5
  199.6 6.6 %collective-permute-start.2 = (f16[24,4096]{1,0:T(8,128)(2,1)S(1)}, f16[24,4096]{1,0:T(8,128)(2,1)S(1)}, u32[]{:S(2)}, u32[]{:S(2)}) collective-permute-start(f16[24,4096]{1,0:T(8,128)(2,1)S(1)} %get-tuple-element.36), channel_id=1, source_target_pairs={{0,4},{1,5},{2,6},{3,7},{4,0},{5,1},{6,2},{7,3},{8,12},{9,13},{10,... | collective-permute-start | bytes 589832 | tf_op jit(solution)/shard_map/ppermute | solution.py:25
  206.2 12.6 %collective-permute-done.6 = f16[24,4096]{1,0:T(8,128)(2,1)S(1)} collective-permute-done((f16[24,4096]{1,0:T(8,128)(2,1)S(1)}, f16[24,4096]{1,0:T(8,128)(2,1)S(1)}, u32[]{:S(2)}, u32[]{:S(2)}) %collective-permute-start.6) | collective-permute-done | bytes 196640 | tf_op jit(solution)/shard_map/ppermute | solution.py:25
  218.9 7.1 %collective-permute-done.2 = f16[24,4096]{1,0:T(8,128)(2,1)S(1)} collective-permute-done((f16[24,4096]{1,0:T(8,128)(2,1)S(1)}, f16[24,4096]{1,0:T(8,128)(2,1)S(1)}, u32[]{:S(2)}, u32[]{:S(2)}) %collective-permute-start.2) | collective-permute-done | bytes 196640 | tf_op jit(solution)/shard_map/ppermute | solution.py:25
  228.5 13.4 %collective-permute-done.9 = f32[24,4096]{1,0:T(8,128)S(1)} collective-permute-done((f32[24,4096]{1,0:T(8,128)S(1)}, f32[24,4096]{1,0:T(8,128)S(1)}, u32[]{:S(2)}, u32[]{:S(2)}) %collective-permute-start.9) | collective-permute-done | bytes 393248 | tf_op jit(solution)/shard_map/ppermute | solution.py:90
  243.7 5.4 %fusion.12 = f32[8192,128]{1,0:T(8,128)} fusion(f32[192]{0:T(256)S(1)} %bitcast.143, bf16[192,4096]{1,0:T(8,128)(2,1)} %all-gather.7.cloned.1.call-done, bf16[1,192,8192]{2,1,0:T(8,128)(2,1)} %all-gather.11.cloned.1.call-done), kind=kOutput, calls=%fused_computation.20 | convolution fusion | flops 407371776 | bytes 7389952 | tf_op jit(solution)/shard_map/dot_general | solution.py:96
  249.3 32.2 %all-gather.9.cloned.1.call-done = bf16[192,4096]{1,0:T(8,128)(2,1)} async-done(((bf16[48,4096]{1,0:T(8,128)(2,1)}), bf16[192,4096]{1,0:T(8,128)(2,1)}) %all-gather.9.cloned.1.call-update) | async-done | bytes 1572880 | tf_op jit(solution)/shard_map/all_gather | solution.py:54
  281.4 21.3 %fusion.4 = f32[192,4096]{1,0:T(8,128)} fusion(bf16[192,4096]{1,0:T(8,128)(2,1)} %all-gather.9.cloned.1.call-done, bf16[8192,4096]{1,0:T(8,128)(2,1)} %param.5), kind=kOutput, calls=%fused_computation.4 | convolution fusion | flops 6442450944 | bytes 38273024 | tf_op jit(solution)/shard_map/dot_general | solution.py:62
  302.8 41.2 %all-gather.13.cloned.1.call-done = bf16[1,192,8192]{2,1,0:T(8,128)(2,1)} async-done(((bf16[1,24,8192]{2,1,0:T(8,128)(2,1)}), bf16[1,192,8192]{2,1,0:T(8,128)(2,1)}) %all-gather.13.cloned.1.call-update) | async-done | bytes 3145744 | tf_op jit(solution)/shard_map/all_gather | solution.py:59
  344.0 20.1 %multiply_reduce_fusion = (f32[192]{0:T(256)S(1)}, f32[192]{0:T(256)S(1)}, f32[192,4096]{1,0:T(8,128)}, f32[192,4096]{1,0:T(8,128)}) fusion(bf16[192,8192]{1,0:T(8,128)(2,1)} %bitcast.148, f32[192,4096]{1,0:T(8,128)} %fusion.4, f32[192]{0:T(256)S(1)} %multiply_divide_fusion, bf16[192,4096]{1,0:T(8,128)(2,1)S(1)} %copy-done.7, bf16[8192,4096]{1,0:T(8,128)(2,1)} %param.5), kind=kOutput, calls=%fused_computation.16 | convolution fusion | flops 6448742400 | bytes 47712512 | tf_op jit(solution)/shard_map/dot_general | solution.py:62
  364.1 39.2 %psum.15 = f32[192]{0:T(256)S(1)} all-reduce(f32[192]{0:T(256)S(1)} %add.236), channel_id=1, replica_groups=mesh['row'=4,'col'=8] {'row','col'}, use_global_device_ids=true, to_apply=%region_7.8 | all-reduce | flops 192 | bytes 1536 | tf_op jit(solution)/shard_map/psum | solution.py:75
  403.3 1.6 fusion.15
  406.5 2.3 collective-permute-start.14
  408.9 6.6 %fusion.9 = f32[8192,128]{1,0:T(8,128)} fusion(f32[8192,128]{1,0:T(8,128)} %fusion.12, f32[192]{0:T(256)S(1)} %psum.15, bf16[8192,4096]{1,0:T(8,128)(2,1)} %param.5, bf16[192,4096]{1,0:T(8,128)(2,1)S(1)} %copy-done.7, bf16[1,192,8192]{2,1,0:T(8,128)(2,1)S(1)} %copy-done.5), kind=kOutput, calls=%fused_computation.10 | convolution fusion | flops 411566080 | bytes 13681664 | tf_op jit(solution)/shard_map/dot_general | solution.py:96
  415.6 11.8 %collective-permute-done.14 = f16[4,24,4096]{2,1,0:T(8,128)(2,1)S(1)} collective-permute-done((f16[4,24,4096]{2,1,0:T(8,128)(2,1)S(1)}, f16[4,24,4096]{2,1,0:T(8,128)(2,1)S(1)}, u32[]{:S(2)}, u32[]{:S(2)}) %collective-permute-start.14) | collective-permute-done | bytes 786464 | tf_op jit(solution)/shard_map/ppermute | solution.py:18
  428.3 3.2 collective-permute-start.17
  431.6 10.9 %collective-permute-done.10 = f16[4,24,4096]{2,1,0:T(8,128)(2,1)S(1)} collective-permute-done((f16[4,24,4096]{2,1,0:T(8,128)(2,1)S(1)}, f16[4,24,4096]{2,1,0:T(8,128)(2,1)S(1)}, u32[]{:S(2)}, u32[]{:S(2)}) %collective-permute-start.10) | collective-permute-done | bytes 786464 | tf_op jit(solution)/shard_map/ppermute | solution.py:18
  443.5 3.3 collective-permute-start.13
  446.9 5.7 %collective-permute-done.11 = f16[24,4096]{1,0:T(8,128)(2,1)S(1)} collective-permute-done((f16[24,4096]{1,0:T(8,128)(2,1)S(1)}, f16[24,4096]{1,0:T(8,128)(2,1)S(1)}, u32[]{:S(2)}, u32[]{:S(2)}) %collective-permute-start.11) | collective-permute-done | bytes 196640 | tf_op jit(solution)/shard_map/ppermute | solution.py:25
  453.5 8.0 %collective-permute-done.12 = f16[24,4096]{1,0:T(8,128)(2,1)S(1)} collective-permute-done((f16[24,4096]{1,0:T(8,128)(2,1)S(1)}, f16[24,4096]{1,0:T(8,128)(2,1)S(1)}, u32[]{:S(2)}, u32[]{:S(2)}) %collective-permute-start.12) | collective-permute-done | bytes 196640 | tf_op jit(solution)/shard_map/ppermute | solution.py:25
  (76 shorter events, 16.1 us)
Async XLA Ops:
  7.2 1.2 copy-start
  7.2 25.9 %all-gather.7.cloned.1.call-start = ((), (), s32[]{:S(2)}) async-start(), calls=%async_computation | async-start | bytes 1966080 | tf_op jit(solution)/shard_map/all_gather | solution.py:54
  10.6 85.7 %all-gather.11.cloned.1.call-start = ((), (), s32[]{:S(2)}) async-start(), calls=%async_computation.2 | async-start | bytes 3538944 | tf_op jit(solution)/shard_map/all_gather | solution.py:41
  12.7 268.8 %all-gather.9.cloned.1.call-start = ((), (), s32[]{:S(2)}) async-start(), calls=%async_computation.1 | async-start | bytes 1966080 | tf_op jit(solution)/shard_map/all_gather | solution.py:54
  33.1 63.2 %copy-start.6 = (bf16[192,4096]{1,0:T(8,128)(2,1)S(1)}, bf16[192,4096]{1,0:T(8,128)(2,1)}, u32[]{:S(2)}) copy-start(bf16[192,4096]{1,0:T(8,128)(2,1)} %all-gather.7.cloned.1.call-done) | copy-start | bytes 4718596
  118.8 69.1 %collective-permute-start.4 = (f16[4,24,4096]{2,1,0:T(8,128)(2,1)}, f16[4,24,4096]{2,1,0:T(8,128)(2,1)S(1)}, u32[]{:S(2)}, u32[]{:S(2)}) collective-permute-start(f16[4,24,4096]{2,1,0:T(8,128)(2,1)} %fusion.14), channel_id=1, source_target_pairs={{0,1},{1,0},{2,3},{3,2},{4,5},{5,4},{6,7},{7,6},{8,9},{9,8},{10,11... | collective-permute-start | bytes 2359304 | tf_op jit(solution)/shard_map/ppermute | solution.py:18
  120.9 72.9 %collective-permute-start = (f16[4,24,4096]{2,1,0:T(8,128)(2,1)S(1)}, f16[4,24,4096]{2,1,0:T(8,128)(2,1)S(1)}, u32[]{:S(2)}, u32[]{:S(2)}) collective-permute-start(f16[4,24,4096]{2,1,0:T(8,128)(2,1)S(1)} %fusion.13), channel_id=1, source_target_pairs={{0,1},{1,0},{2,3},{3,2},{4,5},{5,4},{6,7},{7,6},{8,9},{9,8},{10,11... | collective-permute-start | bytes 2359304 | tf_op jit(solution)/shard_map/ppermute | solution.py:18
  187.9 5.9 %copy-start.2 = (f32[192,4096]{1,0:T(8,128)S(1)}, f32[192,4096]{1,0:T(8,128)}, u32[]{:S(2)}) copy-start(f32[192,4096]{1,0:T(8,128)} %get-tuple-element.18) | copy-start | bytes 9437188
  189.9 9.7 %collective-permute-start.5 = (f16[24,4096]{1,0:T(8,128)(2,1)S(1)}, f16[24,4096]{1,0:T(8,128)(2,1)S(1)}, u32[]{:S(2)}, u32[]{:S(2)}) collective-permute-start(f16[24,4096]{1,0:T(8,128)(2,1)S(1)} %get-tuple-element.37), channel_id=1, source_target_pairs={{0,2},{1,3},{2,4},{3,5},{4,6},{5,7},{6,0},{7,1},{8,10},{9,11},{10,... | collective-permute-start | bytes 589832 | tf_op jit(solution)/shard_map/ppermute | solution.py:25
  190.8 15.3 %collective-permute-start.7 = (f16[24,4096]{1,0:T(8,128)(2,1)S(1)}, f16[24,4096]{1,0:T(8,128)(2,1)S(1)}, u32[]{:S(2)}, u32[]{:S(2)}) collective-permute-start(f16[24,4096]{1,0:T(8,128)(2,1)S(1)} %get-tuple-element.38), channel_id=1, source_target_pairs={{0,6},{1,7},{2,0},{3,1},{4,2},{5,3},{6,4},{7,5},{8,14},{9,15},{10,... | collective-permute-start | bytes 589832 | tf_op jit(solution)/shard_map/ppermute | solution.py:25
  193.8 25.0 %collective-permute-start.6 = (f16[24,4096]{1,0:T(8,128)(2,1)S(1)}, f16[24,4096]{1,0:T(8,128)(2,1)S(1)}, u32[]{:S(2)}, u32[]{:S(2)}) collective-permute-start(f16[24,4096]{1,0:T(8,128)(2,1)S(1)} %get-tuple-element.39), channel_id=1, source_target_pairs={{0,4},{1,5},{2,6},{3,7},{4,0},{5,1},{6,2},{7,3},{8,12},{9,13},{10,... | collective-permute-start | bytes 589832 | tf_op jit(solution)/shard_map/ppermute | solution.py:25
  194.2 24.7 %collective-permute-start.1 = (f16[24,4096]{1,0:T(8,128)(2,1)S(1)}, f16[24,4096]{1,0:T(8,128)(2,1)S(1)}, u32[]{:S(2)}, u32[]{:S(2)}) collective-permute-start(f16[24,4096]{1,0:T(8,128)(2,1)S(1)} %get-tuple-element.34), channel_id=1, source_target_pairs={{0,2},{1,3},{2,4},{3,5},{4,6},{5,7},{6,0},{7,1},{8,10},{9,11},{10,... | collective-permute-start | bytes 589832 | tf_op jit(solution)/shard_map/ppermute | solution.py:25
  194.8 24.1 %collective-permute-start.3 = (f16[24,4096]{1,0:T(8,128)(2,1)S(1)}, f16[24,4096]{1,0:T(8,128)(2,1)S(1)}, u32[]{:S(2)}, u32[]{:S(2)}) collective-permute-start(f16[24,4096]{1,0:T(8,128)(2,1)S(1)} %get-tuple-element.35), channel_id=1, source_target_pairs={{0,6},{1,7},{2,0},{3,1},{4,2},{5,3},{6,4},{7,5},{8,14},{9,15},{10,... | collective-permute-start | bytes 589832 | tf_op jit(solution)/shard_map/ppermute | solution.py:25
  199.6 26.4 %collective-permute-start.2 = (f16[24,4096]{1,0:T(8,128)(2,1)S(1)}, f16[24,4096]{1,0:T(8,128)(2,1)S(1)}, u32[]{:S(2)}, u32[]{:S(2)}) collective-permute-start(f16[24,4096]{1,0:T(8,128)(2,1)S(1)} %get-tuple-element.36), channel_id=1, source_target_pairs={{0,4},{1,5},{2,6},{3,7},{4,0},{5,1},{6,2},{7,3},{8,12},{9,13},{10,... | collective-permute-start | bytes 589832 | tf_op jit(solution)/shard_map/ppermute | solution.py:25
  226.2 15.6 %collective-permute-start.9 = (f32[24,4096]{1,0:T(8,128)S(1)}, f32[24,4096]{1,0:T(8,128)S(1)}, u32[]{:S(2)}, u32[]{:S(2)}) collective-permute-start(f32[24,4096]{1,0:T(8,128)S(1)} %get-tuple-element.32), channel_id=1, source_target_pairs={{0,1},{1,0},{2,9},{3,8},{4,17},{5,16},{6,25},{7,24},{8,3},{9,2},{1... | collective-permute-start | bytes 1179656 | tf_op jit(solution)/shard_map/ppermute | solution.py:90
  227.7 14.2 %collective-permute-start.8 = (f32[24,4096]{1,0:T(8,128)S(1)}, f32[24,4096]{1,0:T(8,128)S(1)}, u32[]{:S(2)}, u32[]{:S(2)}) collective-permute-start(f32[24,4096]{1,0:T(8,128)S(1)} %get-tuple-element.33), channel_id=1, source_target_pairs={{0,0},{1,1},{2,8},{3,9},{4,16},{5,17},{6,24},{7,25},{8,2},{9,3},{1... | collective-permute-start | bytes 1179656 | tf_op jit(solution)/shard_map/ppermute | solution.py:90
  243.1 100.8 %all-gather.13.cloned.1.call-start = ((), (), s32[]{:S(2)}) async-start(), calls=%async_computation.3 | async-start | bytes 3538944 | tf_op jit(solution)/shard_map/all_gather | solution.py:59
  281.4 62.5 %copy-start.7 = (bf16[192,4096]{1,0:T(8,128)(2,1)S(1)}, bf16[192,4096]{1,0:T(8,128)(2,1)}, u32[]{:S(2)}) copy-start(bf16[192,4096]{1,0:T(8,128)(2,1)} %all-gather.9.cloned.1.call-done) | copy-start | bytes 4718596
  403.3 5.7 %copy-start.5 = (bf16[1,192,8192]{2,1,0:T(8,128)(2,1)S(1)}, bf16[1,192,8192]{2,1,0:T(8,128)(2,1)}, u32[]{:S(2)}) copy-start(bf16[1,192,8192]{2,1,0:T(8,128)(2,1)} %all-gather.13.cloned.1.call-done) | copy-start | bytes 9437188
  406.5 20.8 %copy-start.4 = (f32[192,4096]{1,0:T(8,128)S(1)}, f32[192,4096]{1,0:T(8,128)}, u32[]{:S(2)}) copy-start(f32[192,4096]{1,0:T(8,128)} %get-tuple-element.17) | copy-start | bytes 9437188
  406.5 20.8 %collective-permute-start.14 = (f16[4,24,4096]{2,1,0:T(8,128)(2,1)S(1)}, f16[4,24,4096]{2,1,0:T(8,128)(2,1)S(1)}, u32[]{:S(2)}, u32[]{:S(2)}) collective-permute-start(f16[4,24,4096]{2,1,0:T(8,128)(2,1)S(1)} %fusion.16), channel_id=1, source_target_pairs={{0,1},{1,0},{2,3},{3,2},{4,5},{5,4},{6,7},{7,6},{8,9},{9,8},{10,11... | collective-permute-start | bytes 2359304 | tf_op jit(solution)/shard_map/ppermute | solution.py:18
  408.9 33.6 %collective-permute-start.10 = (f16[4,24,4096]{2,1,0:T(8,128)(2,1)S(1)}, f16[4,24,4096]{2,1,0:T(8,128)(2,1)S(1)}, u32[]{:S(2)}, u32[]{:S(2)}) collective-permute-start(f16[4,24,4096]{2,1,0:T(8,128)(2,1)S(1)} %fusion.15), channel_id=1, source_target_pairs={{0,1},{1,0},{2,3},{3,2},{4,5},{5,4},{6,7},{7,6},{8,9},{9,8},{10,11... | collective-permute-start | bytes 2359304 | tf_op jit(solution)/shard_map/ppermute | solution.py:18
  415.6 26.9 %copy-start.3 = (f32[192,4096]{1,0:T(8,128)S(1)}, f32[192,4096]{1,0:T(8,128)}, u32[]{:S(2)}) copy-start(f32[192,4096]{1,0:T(8,128)} %get-tuple-element.16) | copy-start | bytes 9437188
  427.7 19.1 %collective-permute-start.15 = (f16[24,4096]{1,0:T(8,128)(2,1)S(1)}, f16[24,4096]{1,0:T(8,128)(2,1)S(1)}, u32[]{:S(2)}, u32[]{:S(2)}) collective-permute-start(f16[24,4096]{1,0:T(8,128)(2,1)S(1)} %get-tuple-element.29), channel_id=1, source_target_pairs={{0,2},{1,3},{2,4},{3,5},{4,6},{5,7},{6,0},{7,1},{8,10},{9,11},{10,... | collective-permute-start | bytes 589832 | tf_op jit(solution)/shard_map/ppermute | solution.py:25
  428.3 18.4 %collective-permute-start.17 = (f16[24,4096]{1,0:T(8,128)(2,1)S(1)}, f16[24,4096]{1,0:T(8,128)(2,1)S(1)}, u32[]{:S(2)}, u32[]{:S(2)}) collective-permute-start(f16[24,4096]{1,0:T(8,128)(2,1)S(1)} %get-tuple-element.30), channel_id=1, source_target_pairs={{0,6},{1,7},{2,0},{3,1},{4,2},{5,3},{6,4},{7,5},{8,14},{9,15},{10,... | collective-permute-start | bytes 589832 | tf_op jit(solution)/shard_map/ppermute | solution.py:25
  431.6 15.2 %collective-permute-start.16 = (f16[24,4096]{1,0:T(8,128)(2,1)S(1)}, f16[24,4096]{1,0:T(8,128)(2,1)S(1)}, u32[]{:S(2)}, u32[]{:S(2)}) collective-permute-start(f16[24,4096]{1,0:T(8,128)(2,1)S(1)} %get-tuple-element.31), channel_id=1, source_target_pairs={{0,4},{1,5},{2,6},{3,7},{4,0},{5,1},{6,2},{7,3},{8,12},{9,13},{10,... | collective-permute-start | bytes 589832 | tf_op jit(solution)/shard_map/ppermute | solution.py:25
  442.9 9.7 %collective-permute-start.11 = (f16[24,4096]{1,0:T(8,128)(2,1)S(1)}, f16[24,4096]{1,0:T(8,128)(2,1)S(1)}, u32[]{:S(2)}, u32[]{:S(2)}) collective-permute-start(f16[24,4096]{1,0:T(8,128)(2,1)S(1)} %get-tuple-element.26), channel_id=1, source_target_pairs={{0,2},{1,3},{2,4},{3,5},{4,6},{5,7},{6,0},{7,1},{8,10},{9,11},{10,... | collective-permute-start | bytes 589832 | tf_op jit(solution)/shard_map/ppermute | solution.py:25
  443.5 10.0 %collective-permute-start.13 = (f16[24,4096]{1,0:T(8,128)(2,1)S(1)}, f16[24,4096]{1,0:T(8,128)(2,1)S(1)}, u32[]{:S(2)}, u32[]{:S(2)}) collective-permute-start(f16[24,4096]{1,0:T(8,128)(2,1)S(1)} %get-tuple-element.27), channel_id=1, source_target_pairs={{0,6},{1,7},{2,0},{3,1},{4,2},{5,3},{6,4},{7,5},{8,14},{9,15},{10,... | collective-permute-start | bytes 589832 | tf_op jit(solution)/shard_map/ppermute | solution.py:25
  446.8 14.7 %collective-permute-start.12 = (f16[24,4096]{1,0:T(8,128)(2,1)S(1)}, f16[24,4096]{1,0:T(8,128)(2,1)S(1)}, u32[]{:S(2)}, u32[]{:S(2)}) collective-permute-start(f16[24,4096]{1,0:T(8,128)(2,1)S(1)} %get-tuple-element.28), channel_id=1, source_target_pairs={{0,4},{1,5},{2,6},{3,7},{4,0},{5,1},{6,2},{7,3},{8,12},{9,13},{10,... | collective-permute-start | bytes 589832 | tf_op jit(solution)/shard_map/ppermute | solution.py:25
  446.8 16.2 %copy-start.1 = (bf16[96,4096]{1,0:T(8,128)(2,1)S(1)}, bf16[96,4096]{1,0:T(8,128)(2,1)}, u32[]{:S(2)}) copy-start(bf16[96,4096]{1,0:T(8,128)(2,1)} %param.6) | copy-start | bytes 2359300
Sparse Core Ops, SparseCore 0:
  10.7 22.3 all-gather.6
  35.8 60.4 all-gather.10
  243.3 38.1 all-gather.8
  283.5 60.4 all-gather.12
where the time goes:
time: 470 us; the launch traced here: 469 us
  waiting for transfers between devices  208 us (44%)
  blocking collectives  105 us (22%)
  matrix products  98.1 us (21%)
  starting transfers between devices  29 us (6%)
  between operations  14.1 us (3%)
  other arithmetic  11.9 us (3%)
    dot_general x4, matrix products, on_device(): lax.dot_general(weighted_back, transition[rows], (((1,), (1,)), ((), ()))...  82.8 us
    psum x1, blocking collectives, on_device(): both = lax.psum(jnp.stack([norm, mass]), ('row', 'col'))  65.4 us
    all_gather x2, waiting for transfers between devices, on_device(): weighted_back = lax.all_gather(local_back, 'row', axis=0, tiled=True)  52.4 us
    all_gather x1, waiting for transfers between devices, on_device(): forward_all = [None, lax.all_gather(forward[1], 'col', axis=0, tiled=True)]  42 us
    all_gather x1, waiting for transfers between devices, on_device(): forward_all[0] = lax.all_gather(forward[0], 'col', axis=0, tiled=True)  41.2 us
    psum x1, blocking collectives, on_device(): normal_all = lax.psum(norm, ('row', 'col'))  39.2 us
    ppermute x12, waiting for transfers between devices, reduce_scatter(): lax.ppermute(piece, 'col', [(c, (c + 2 * k) % col_count) for c in range(c...  35.8 us
    ppermute x4, waiting for transfers between devices, reduce_scatter(): got = lax.ppermute(away, 'col', [(c, c ^ 1) for c in range(col_count)])  22.7 us
  transfers between devices with their start and end apart: 22, of which 13 were waited for; matrix products, arithmetic and copies ran while one was open for 13% of the time, Pallas kernels for 0%

commit v1 on v0

--- a/solution.py
+++ b/solution.py
@@ -69,7 +69,9 @@
             mass = mass + jnp.sum(partial, axis=1)
             pieces.append(reduce_scatter(partial, scale, col_count, col_index, local_seqs))
         if step == 1:
-            both = lax.psum(jnp.stack([norm, mass]), ("row", "col"))
+            both = jnp.stack([norm, mass])
+            for mesh_axis in ("col", "row"):
+                both = lax.psum(both, mesh_axis)
             normal_all = both[0]
         else:
             normal_all = lax.psum(norm, ("row", "col"))

time: 470 us -> 454 us (0.966)
  blocking collectives: 105 us -> 89.3 us
  waiting for transfers between devices: 208 us -> 215 us
  starting transfers between devices: 29 us -> 22.1 us
    psum x1 -> x2, blocking collectives: 65.4 us -> 50.1 us  [on_device(): both = lax.psum(both, mesh_axis)]
    ppermute x12, starting transfers between devices: 22.1 us -> 15.5 us  [reduce_scatter(): lax.ppermute(piece, 'col', [(c, (c + 2 * k) % col_count) for c in range(c...]
    ppermute x12, waiting for transfers between devices: 35.8 us -> 40.9 us  [reduce_scatter(): lax.ppermute(piece, 'col', [(c, (c + 2 * k) % col_count) for c in range(c...]
  transfers between devices with their start and end apart: 22 -> 22, of which waited for: 13 -> 15; matrix products, arithmetic and copies ran while one was open for 13% -> 14% of each run, Pallas kernels for 0% -> 0%
where the time goes in v1:
time: 454 us
  waiting for transfers between devices  215 us (47%)
  matrix products  98.2 us (22%)
  blocking collectives  89.3 us (20%)
  starting transfers between devices  22.1 us (5%)
  between operations  14.1 us (3%)
  other arithmetic  11.9 us (3%)
    dot_general x4, matrix products, on_device(): lax.dot_general(weighted_back, transition[rows], (((1,), (1,)), ((), ()))...  82.9 us
    all_gather x2, waiting for transfers between devices, on_device(): weighted_back = lax.all_gather(local_back, 'row', axis=0, tiled=True)  53 us
    psum x2, blocking collectives, on_device(): both = lax.psum(both, mesh_axis)  50.1 us
    all_gather x1, waiting for transfers between devices, on_device(): forward_all = [None, lax.all_gather(forward[1], 'col', axis=0, tiled=True)]  42 us
    all_gather x1, waiting for transfers between devices, on_device(): forward_all[0] = lax.all_gather(forward[0], 'col', axis=0, tiled=True)  41.1 us
    ppermute x12, waiting for transfers between devices, reduce_scatter(): lax.ppermute(piece, 'col', [(c, (c + 2 * k) % col_count) for c in range(c...  40.9 us
    psum x1, blocking collectives, on_device(): normal_all = lax.psum(norm, ('row', 'col'))  39.2 us
    ppermute x4, waiting for transfers between devices, reduce_scatter(): got = lax.ppermute(away, 'col', [(c, c ^ 1) for c in range(col_count)])  22.7 us
  transfers between devices with their start and end apart: 22, of which 15 were waited for; matrix products, arithmetic and copies ran while one was open for 14% of the time, Pallas kernels for 0%

profile of v1, /device:TPU:0, one launch (start us, length us, event | category | flops | bytes accessed | tf_op | source)
XLA Modules:
  0.0 453.9 jit_solution(10848012479626981116)
XLA Ops:
  8.3 2.2 fusion.10
  10.6 2.0 fusion.50
  12.8 20.2 %all-gather.7.cloned.1.call-done = bf16[192,4096]{1,0:T(8,128)(2,1)} async-done(((bf16[48,4096]{1,0:T(8,128)(2,1)}), bf16[192,4096]{1,0:T(8,128)(2,1)}) %all-gather.7.cloned.1.call-update) | async-done | bytes 1572880 | tf_op jit(solution)/shard_map/all_gather | solution.py:54
  33.1 21.2 %fusion.6 = f32[192,4096]{1,0:T(8,128)} fusion(bf16[192,4096]{1,0:T(8,128)(2,1)} %all-gather.7.cloned.1.call-done, bf16[8192,4096]{1,0:T(8,128)(2,1)} %param.5), kind=kOutput, calls=%fused_computation.6 | convolution fusion | flops 6442450944 | bytes 38273024 | tf_op jit(solution)/shard_map/dot_general | solution.py:62
  54.3 42.0 %all-gather.11.cloned.1.call-done = bf16[1,192,8192]{2,1,0:T(8,128)(2,1)} async-done(((bf16[1,24,8192]{2,1,0:T(8,128)(2,1)}), bf16[1,192,8192]{2,1,0:T(8,128)(2,1)}) %all-gather.11.cloned.1.call-update) | async-done | bytes 3145744 | tf_op jit(solution)/shard_map/all_gather | solution.py:41
  96.3 20.1 %multiply_reduce_fusion.2 = (f32[192]{0:T(256)S(1)}, f32[192]{0:T(256)S(1)}, f32[192]{0:T(256)S(1)}, f32[192]{0:T(256)S(1)}, f32[192,4096]{1,0:T(8,128)}, /*index=5*/f32[192,4096]{1,0:T(8,128)}) fusion(bf16[192,8192]{1,0:T(8,128)(2,1)} %bitcast.147, f32[192,4096]{1,0:T(8,128)} %fusion.6, bf16[192,4096]{1,0:T(8,128)(2,1)S(1)} %copy-done.6, ...), kind=kOutput, calls=%fused_computation.18 | convolution fusion | flops 6450315264 | bytes 47713280 | tf_op jit(solution)/shard_map/dot_general | solution.py:62
  116.4 2.4 fusion.14
  120.8 1.5 collective-permute-start
  122.4 44.4 %psum.21 = f32[2,192]{1,0:T(2,128)S(1)} all-reduce(f32[2,192]{1,0:T(2,128)S(1)} %pad_maximum_fusion.1), channel_id=1, replica_groups=mesh['row'=4,'col'=8] {'col'}, use_global_device_ids=true, to_apply=%region_4.5 | all-reduce | flops 384 | bytes 3072 | tf_op jit(solution)/shard_map/psum | solution.py:74
  166.8 5.6 %psum.22 = f32[2,192]{1,0:T(2,128)S(1)} all-reduce(f32[2,192]{1,0:T(2,128)S(1)} %psum.21), channel_id=1, replica_groups=mesh['row'=4,'col'=8] {'row'}, use_global_device_ids=true, to_apply=%region_5.6 | all-reduce | flops 384 | bytes 3072 | tf_op jit(solution)/shard_map/psum | solution.py:74
  172.6 1.8 fusion.49
  174.6 3.8 collective-permute-start.7
  179.4 3.3 collective-permute-start.3
  184.1 6.2 %collective-permute-done.7 = f16[24,4096]{1,0:T(8,128)(2,1)S(1)} collective-permute-done((f16[24,4096]{1,0:T(8,128)(2,1)S(1)}, f16[24,4096]{1,0:T(8,128)(2,1)S(1)}, u32[]{:S(2)}, u32[]{:S(2)}) %collective-permute-start.7) | collective-permute-done | bytes 196640 | tf_op jit(solution)/shard_map/ppermute | solution.py:25
  190.3 6.6 %collective-permute-done.6 = f16[24,4096]{1,0:T(8,128)(2,1)S(1)} collective-permute-done((f16[24,4096]{1,0:T(8,128)(2,1)S(1)}, f16[24,4096]{1,0:T(8,128)(2,1)S(1)}, u32[]{:S(2)}, u32[]{:S(2)}) %collective-permute-start.6) | collective-permute-done | bytes 196640 | tf_op jit(solution)/shard_map/ppermute | solution.py:25
  198.1 10.9 %collective-permute-done.2 = f16[24,4096]{1,0:T(8,128)(2,1)S(1)} collective-permute-done((f16[24,4096]{1,0:T(8,128)(2,1)S(1)}, f16[24,4096]{1,0:T(8,128)(2,1)S(1)}, u32[]{:S(2)}, u32[]{:S(2)}) %collective-permute-start.2) | collective-permute-done | bytes 196640 | tf_op jit(solution)/shard_map/ppermute | solution.py:25
  211.1 14.5 %collective-permute-done.9 = f32[24,4096]{1,0:T(8,128)S(1)} collective-permute-done((f32[24,4096]{1,0:T(8,128)S(1)}, f32[24,4096]{1,0:T(8,128)S(1)}, u32[]{:S(2)}, u32[]{:S(2)}) %collective-permute-start.9) | collective-permute-done | bytes 393248 | tf_op jit(solution)/shard_map/ppermute | solution.py:92
  227.4 5.4 %fusion.12 = f32[8192,128]{1,0:T(8,128)} fusion(f32[192]{0:T(256)S(1)} %bitcast.143, bf16[192,4096]{1,0:T(8,128)(2,1)} %all-gather.7.cloned.1.call-done, bf16[1,192,8192]{2,1,0:T(8,128)(2,1)} %all-gather.11.cloned.1.call-done), kind=kOutput, calls=%fused_computation.20 | convolution fusion | flops 407371776 | bytes 7389952 | tf_op jit(solution)/shard_map/dot_general | solution.py:98
  233.0 32.8 %all-gather.9.cloned.1.call-done = bf16[192,4096]{1,0:T(8,128)(2,1)} async-done(((bf16[48,4096]{1,0:T(8,128)(2,1)}), bf16[192,4096]{1,0:T(8,128)(2,1)}) %all-gather.9.cloned.1.call-update) | async-done | bytes 1572880 | tf_op jit(solution)/shard_map/all_gather | solution.py:54
  265.8 21.4 %fusion.4 = f32[192,4096]{1,0:T(8,128)} fusion(bf16[192,4096]{1,0:T(8,128)(2,1)} %all-gather.9.cloned.1.call-done, bf16[8192,4096]{1,0:T(8,128)(2,1)} %param.5), kind=kOutput, calls=%fused_computation.4 | convolution fusion | flops 6442450944 | bytes 38273024 | tf_op jit(solution)/shard_map/dot_general | solution.py:62
  287.2 41.1 %all-gather.13.cloned.1.call-done = bf16[1,192,8192]{2,1,0:T(8,128)(2,1)} async-done(((bf16[1,24,8192]{2,1,0:T(8,128)(2,1)}), bf16[1,192,8192]{2,1,0:T(8,128)(2,1)}) %all-gather.13.cloned.1.call-update) | async-done | bytes 3145744 | tf_op jit(solution)/shard_map/all_gather | solution.py:59
  328.3 20.2 %multiply_reduce_fusion = (f32[192]{0:T(256)S(1)}, f32[192]{0:T(256)S(1)}, f32[192,4096]{1,0:T(8,128)}, f32[192,4096]{1,0:T(8,128)}) fusion(bf16[192,8192]{1,0:T(8,128)(2,1)} %bitcast.148, f32[192,4096]{1,0:T(8,128)} %fusion.4, f32[192]{0:T(256)S(1)} %multiply_divide_fusion, bf16[192,4096]{1,0:T(8,128)(2,1)S(1)} %copy-done.7, bf16[8192,4096]{1,0:T(8,128)(2,1)} %param.5), kind=kOutput, calls=%fused_computation.16 | convolution fusion | flops 6448742400 | bytes 47712512 | tf_op jit(solution)/shard_map/dot_general | solution.py:62
  348.5 39.2 %psum.23 = f32[192]{0:T(256)S(1)} all-reduce(f32[192]{0:T(256)S(1)} %add.238), channel_id=1, replica_groups=mesh['row'=4,'col'=8] {'row','col'}, use_global_device_ids=true, to_apply=%region_8.9 | all-reduce | flops 192 | bytes 1536 | tf_op jit(solution)/shard_map/psum | solution.py:77
  387.7 1.6 fusion.15
  390.9 2.3 collective-permute-start.14
  393.3 6.6 %fusion.9 = f32[8192,128]{1,0:T(8,128)} fusion(f32[8192,128]{1,0:T(8,128)} %fusion.12, f32[192]{0:T(256)S(1)} %psum.23, bf16[8192,4096]{1,0:T(8,128)(2,1)} %param.5, bf16[192,4096]{1,0:T(8,128)(2,1)S(1)} %copy-done.7, bf16[1,192,8192]{2,1,0:T(8,128)(2,1)S(1)} %copy-done.5), kind=kOutput, calls=%fused_computation.10 | convolution fusion | flops 411566080 | bytes 13681664 | tf_op jit(solution)/shard_map/dot_general | solution.py:98
  400.0 11.7 %collective-permute-done.14 = f16[4,24,4096]{2,1,0:T(8,128)(2,1)S(1)} collective-permute-done((f16[4,24,4096]{2,1,0:T(8,128)(2,1)S(1)}, f16[4,24,4096]{2,1,0:T(8,128)(2,1)S(1)}, u32[]{:S(2)}, u32[]{:S(2)}) %collective-permute-start.14) | collective-permute-done | bytes 786464 | tf_op jit(solution)/shard_map/ppermute | solution.py:18
  412.7 3.2 collective-permute-start.17
  416.0 10.9 %collective-permute-done.10 = f16[4,24,4096]{2,1,0:T(8,128)(2,1)S(1)} collective-permute-done((f16[4,24,4096]{2,1,0:T(8,128)(2,1)S(1)}, f16[4,24,4096]{2,1,0:T(8,128)(2,1)S(1)}, u32[]{:S(2)}, u32[]{:S(2)}) %collective-permute-start.10) | collective-permute-done | bytes 786464 | tf_op jit(solution)/shard_map/ppermute | solution.py:18
  427.9 3.3 collective-permute-start.13
  431.3 5.7 %collective-permute-done.11 = f16[24,4096]{1,0:T(8,128)(2,1)S(1)} collective-permute-done((f16[24,4096]{1,0:T(8,128)(2,1)S(1)}, f16[24,4096]{1,0:T(8,128)(2,1)S(1)}, u32[]{:S(2)}, u32[]{:S(2)}) %collective-permute-start.11) | collective-permute-done | bytes 196640 | tf_op jit(solution)/shard_map/ppermute | solution.py:25
  437.9 8.0 %collective-permute-done.12 = f16[24,4096]{1,0:T(8,128)(2,1)S(1)} collective-permute-done((f16[24,4096]{1,0:T(8,128)(2,1)S(1)}, f16[24,4096]{1,0:T(8,128)(2,1)S(1)}, u32[]{:S(2)}, u32[]{:S(2)}) %collective-permute-start.12) | collective-permute-done | bytes 196640 | tf_op jit(solution)/shard_map/ppermute | solution.py:25
  (77 shorter events, 17.4 us)
Async XLA Ops:
  7.2 1.2 copy-start
  7.2 25.9 %all-gather.7.cloned.1.call-start = ((), (), s32[]{:S(2)}) async-start(), calls=%async_computation | async-start | bytes 1966080 | tf_op jit(solution)/shard_map/all_gather | solution.py:54
  10.6 85.7 %all-gather.11.cloned.1.call-start = ((), (), s32[]{:S(2)}) async-start(), calls=%async_computation.2 | async-start | bytes 3538944 | tf_op jit(solution)/shard_map/all_gather | solution.py:41
  12.7 253.1 %all-gather.9.cloned.1.call-start = ((), (), s32[]{:S(2)}) async-start(), calls=%async_computation.1 | async-start | bytes 1966080 | tf_op jit(solution)/shard_map/all_gather | solution.py:54
  33.1 63.2 %copy-start.6 = (bf16[192,4096]{1,0:T(8,128)(2,1)S(1)}, bf16[192,4096]{1,0:T(8,128)(2,1)}, u32[]{:S(2)}) copy-start(bf16[192,4096]{1,0:T(8,128)(2,1)} %all-gather.7.cloned.1.call-done) | copy-start | bytes 4718596
  118.8 53.8 %collective-permute-start.4 = (f16[4,24,4096]{2,1,0:T(8,128)(2,1)}, f16[4,24,4096]{2,1,0:T(8,128)(2,1)S(1)}, u32[]{:S(2)}, u32[]{:S(2)}) collective-permute-start(f16[4,24,4096]{2,1,0:T(8,128)(2,1)} %fusion.14), channel_id=1, source_target_pairs={{0,1},{1,0},{2,3},{3,2},{4,5},{5,4},{6,7},{7,6},{8,9},{9,8},{10,11... | collective-permute-start | bytes 2359304 | tf_op jit(solution)/shard_map/ppermute | solution.py:18
  120.8 57.5 %collective-permute-start = (f16[4,24,4096]{2,1,0:T(8,128)(2,1)S(1)}, f16[4,24,4096]{2,1,0:T(8,128)(2,1)S(1)}, u32[]{:S(2)}, u32[]{:S(2)}) collective-permute-start(f16[4,24,4096]{2,1,0:T(8,128)(2,1)S(1)} %fusion.13), channel_id=1, source_target_pairs={{0,1},{1,0},{2,3},{3,2},{4,5},{5,4},{6,7},{7,6},{8,9},{9,8},{10,11... | collective-permute-start | bytes 2359304 | tf_op jit(solution)/shard_map/ppermute | solution.py:18
  172.5 5.9 %copy-start.2 = (f32[192,4096]{1,0:T(8,128)S(1)}, f32[192,4096]{1,0:T(8,128)}, u32[]{:S(2)}) copy-start(f32[192,4096]{1,0:T(8,128)} %get-tuple-element.18) | copy-start | bytes 9437188
  174.5 9.6 %collective-permute-start.5 = (f16[24,4096]{1,0:T(8,128)(2,1)S(1)}, f16[24,4096]{1,0:T(8,128)(2,1)S(1)}, u32[]{:S(2)}, u32[]{:S(2)}) collective-permute-start(f16[24,4096]{1,0:T(8,128)(2,1)S(1)} %get-tuple-element.37), channel_id=1, source_target_pairs={{0,2},{1,3},{2,4},{3,5},{4,6},{5,7},{6,0},{7,1},{8,10},{9,11},{10,... | collective-permute-start | bytes 589832 | tf_op jit(solution)/shard_map/ppermute | solution.py:25
  174.6 15.7 %collective-permute-start.7 = (f16[24,4096]{1,0:T(8,128)(2,1)S(1)}, f16[24,4096]{1,0:T(8,128)(2,1)S(1)}, u32[]{:S(2)}, u32[]{:S(2)}) collective-permute-start(f16[24,4096]{1,0:T(8,128)(2,1)S(1)} %get-tuple-element.38), channel_id=1, source_target_pairs={{0,6},{1,7},{2,0},{3,1},{4,2},{5,3},{6,4},{7,5},{8,14},{9,15},{10,... | collective-permute-start | bytes 589832 | tf_op jit(solution)/shard_map/ppermute | solution.py:25
  178.4 18.5 %collective-permute-start.6 = (f16[24,4096]{1,0:T(8,128)(2,1)S(1)}, f16[24,4096]{1,0:T(8,128)(2,1)S(1)}, u32[]{:S(2)}, u32[]{:S(2)}) collective-permute-start(f16[24,4096]{1,0:T(8,128)(2,1)S(1)} %get-tuple-element.39), channel_id=1, source_target_pairs={{0,4},{1,5},{2,6},{3,7},{4,0},{5,1},{6,2},{7,3},{8,12},{9,13},{10,... | collective-permute-start | bytes 589832 | tf_op jit(solution)/shard_map/ppermute | solution.py:25
  178.8 18.2 %collective-permute-start.1 = (f16[24,4096]{1,0:T(8,128)(2,1)S(1)}, f16[24,4096]{1,0:T(8,128)(2,1)S(1)}, u32[]{:S(2)}, u32[]{:S(2)}) collective-permute-start(f16[24,4096]{1,0:T(8,128)(2,1)S(1)} %get-tuple-element.34), channel_id=1, source_target_pairs={{0,2},{1,3},{2,4},{3,5},{4,6},{5,7},{6,0},{7,1},{8,10},{9,11},{10,... | collective-permute-start | bytes 589832 | tf_op jit(solution)/shard_map/ppermute | solution.py:25
  179.4 18.8 %collective-permute-start.3 = (f16[24,4096]{1,0:T(8,128)(2,1)S(1)}, f16[24,4096]{1,0:T(8,128)(2,1)S(1)}, u32[]{:S(2)}, u32[]{:S(2)}) collective-permute-start(f16[24,4096]{1,0:T(8,128)(2,1)S(1)} %get-tuple-element.35), channel_id=1, source_target_pairs={{0,6},{1,7},{2,0},{3,1},{4,2},{5,3},{6,4},{7,5},{8,14},{9,15},{10,... | collective-permute-start | bytes 589832 | tf_op jit(solution)/shard_map/ppermute | solution.py:25
  184.1 24.9 %collective-permute-start.2 = (f16[24,4096]{1,0:T(8,128)(2,1)S(1)}, f16[24,4096]{1,0:T(8,128)(2,1)S(1)}, u32[]{:S(2)}, u32[]{:S(2)}) collective-permute-start(f16[24,4096]{1,0:T(8,128)(2,1)S(1)} %get-tuple-element.36), channel_id=1, source_target_pairs={{0,4},{1,5},{2,6},{3,7},{4,0},{5,1},{6,2},{7,3},{8,12},{9,13},{10,... | collective-permute-start | bytes 589832 | tf_op jit(solution)/shard_map/ppermute | solution.py:25
  209.3 16.3 %collective-permute-start.9 = (f32[24,4096]{1,0:T(8,128)S(1)}, f32[24,4096]{1,0:T(8,128)S(1)}, u32[]{:S(2)}, u32[]{:S(2)}) collective-permute-start(f32[24,4096]{1,0:T(8,128)S(1)} %get-tuple-element.32), channel_id=1, source_target_pairs={{0,1},{1,0},{2,9},{3,8},{4,17},{5,16},{6,25},{7,24},{8,3},{9,2},{1... | collective-permute-start | bytes 1179656 | tf_op jit(solution)/shard_map/ppermute | solution.py:92
  210.3 15.3 %collective-permute-start.8 = (f32[24,4096]{1,0:T(8,128)S(1)}, f32[24,4096]{1,0:T(8,128)S(1)}, u32[]{:S(2)}, u32[]{:S(2)}) collective-permute-start(f32[24,4096]{1,0:T(8,128)S(1)} %get-tuple-element.33), channel_id=1, source_target_pairs={{0,0},{1,1},{2,8},{3,9},{4,16},{5,17},{6,24},{7,25},{8,2},{9,3},{1... | collective-permute-start | bytes 1179656 | tf_op jit(solution)/shard_map/ppermute | solution.py:92
  226.8 101.5 %all-gather.13.cloned.1.call-start = ((), (), s32[]{:S(2)}) async-start(), calls=%async_computation.3 | async-start | bytes 3538944 | tf_op jit(solution)/shard_map/all_gather | solution.py:59
  265.8 62.5 %copy-start.7 = (bf16[192,4096]{1,0:T(8,128)(2,1)S(1)}, bf16[192,4096]{1,0:T(8,128)(2,1)}, u32[]{:S(2)}) copy-start(bf16[192,4096]{1,0:T(8,128)(2,1)} %all-gather.9.cloned.1.call-done) | copy-start | bytes 4718596
  387.7 5.7 %copy-start.5 = (bf16[1,192,8192]{2,1,0:T(8,128)(2,1)S(1)}, bf16[1,192,8192]{2,1,0:T(8,128)(2,1)}, u32[]{:S(2)}) copy-start(bf16[1,192,8192]{2,1,0:T(8,128)(2,1)} %all-gather.13.cloned.1.call-done) | copy-start | bytes 9437188
  390.9 20.8 %copy-start.4 = (f32[192,4096]{1,0:T(8,128)S(1)}, f32[192,4096]{1,0:T(8,128)}, u32[]{:S(2)}) copy-start(f32[192,4096]{1,0:T(8,128)} %get-tuple-element.17) | copy-start | bytes 9437188
  390.9 20.8 %collective-permute-start.14 = (f16[4,24,4096]{2,1,0:T(8,128)(2,1)S(1)}, f16[4,24,4096]{2,1,0:T(8,128)(2,1)S(1)}, u32[]{:S(2)}, u32[]{:S(2)}) collective-permute-start(f16[4,24,4096]{2,1,0:T(8,128)(2,1)S(1)} %fusion.16), channel_id=1, source_target_pairs={{0,1},{1,0},{2,3},{3,2},{4,5},{5,4},{6,7},{7,6},{8,9},{9,8},{10,11... | collective-permute-start | bytes 2359304 | tf_op jit(solution)/shard_map/ppermute | solution.py:18
  393.3 33.6 %collective-permute-start.10 = (f16[4,24,4096]{2,1,0:T(8,128)(2,1)S(1)}, f16[4,24,4096]{2,1,0:T(8,128)(2,1)S(1)}, u32[]{:S(2)}, u32[]{:S(2)}) collective-permute-start(f16[4,24,4096]{2,1,0:T(8,128)(2,1)S(1)} %fusion.15), channel_id=1, source_target_pairs={{0,1},{1,0},{2,3},{3,2},{4,5},{5,4},{6,7},{7,6},{8,9},{9,8},{10,11... | collective-permute-start | bytes 2359304 | tf_op jit(solution)/shard_map/ppermute | solution.py:18
  400.0 26.9 %copy-start.3 = (f32[192,4096]{1,0:T(8,128)S(1)}, f32[192,4096]{1,0:T(8,128)}, u32[]{:S(2)}) copy-start(f32[192,4096]{1,0:T(8,128)} %get-tuple-element.16) | copy-start | bytes 9437188
  412.1 19.1 %collective-permute-start.15 = (f16[24,4096]{1,0:T(8,128)(2,1)S(1)}, f16[24,4096]{1,0:T(8,128)(2,1)S(1)}, u32[]{:S(2)}, u32[]{:S(2)}) collective-permute-start(f16[24,4096]{1,0:T(8,128)(2,1)S(1)} %get-tuple-element.29), channel_id=1, source_target_pairs={{0,2},{1,3},{2,4},{3,5},{4,6},{5,7},{6,0},{7,1},{8,10},{9,11},{10,... | collective-permute-start | bytes 589832 | tf_op jit(solution)/shard_map/ppermute | solution.py:25
  412.7 18.4 %collective-permute-start.17 = (f16[24,4096]{1,0:T(8,128)(2,1)S(1)}, f16[24,4096]{1,0:T(8,128)(2,1)S(1)}, u32[]{:S(2)}, u32[]{:S(2)}) collective-permute-start(f16[24,4096]{1,0:T(8,128)(2,1)S(1)} %get-tuple-element.30), channel_id=1, source_target_pairs={{0,6},{1,7},{2,0},{3,1},{4,2},{5,3},{6,4},{7,5},{8,14},{9,15},{10,... | collective-permute-start | bytes 589832 | tf_op jit(solution)/shard_map/ppermute | solution.py:25
  416.0 15.2 %collective-permute-start.16 = (f16[24,4096]{1,0:T(8,128)(2,1)S(1)}, f16[24,4096]{1,0:T(8,128)(2,1)S(1)}, u32[]{:S(2)}, u32[]{:S(2)}) collective-permute-start(f16[24,4096]{1,0:T(8,128)(2,1)S(1)} %get-tuple-element.31), channel_id=1, source_target_pairs={{0,4},{1,5},{2,6},{3,7},{4,0},{5,1},{6,2},{7,3},{8,12},{9,13},{10,... | collective-permute-start | bytes 589832 | tf_op jit(solution)/shard_map/ppermute | solution.py:25
  427.3 9.7 %collective-permute-start.11 = (f16[24,4096]{1,0:T(8,128)(2,1)S(1)}, f16[24,4096]{1,0:T(8,128)(2,1)S(1)}, u32[]{:S(2)}, u32[]{:S(2)}) collective-permute-start(f16[24,4096]{1,0:T(8,128)(2,1)S(1)} %get-tuple-element.26), channel_id=1, source_target_pairs={{0,2},{1,3},{2,4},{3,5},{4,6},{5,7},{6,0},{7,1},{8,10},{9,11},{10,... | collective-permute-start | bytes 589832 | tf_op jit(solution)/shard_map/ppermute | solution.py:25
  427.9 10.0 %collective-permute-start.13 = (f16[24,4096]{1,0:T(8,128)(2,1)S(1)}, f16[24,4096]{1,0:T(8,128)(2,1)S(1)}, u32[]{:S(2)}, u32[]{:S(2)}) collective-permute-start(f16[24,4096]{1,0:T(8,128)(2,1)S(1)} %get-tuple-element.27), channel_id=1, source_target_pairs={{0,6},{1,7},{2,0},{3,1},{4,2},{5,3},{6,4},{7,5},{8,14},{9,15},{10,... | collective-permute-start | bytes 589832 | tf_op jit(solution)/shard_map/ppermute | solution.py:25
  431.2 14.7 %collective-permute-start.12 = (f16[24,4096]{1,0:T(8,128)(2,1)S(1)}, f16[24,4096]{1,0:T(8,128)(2,1)S(1)}, u32[]{:S(2)}, u32[]{:S(2)}) collective-permute-start(f16[24,4096]{1,0:T(8,128)(2,1)S(1)} %get-tuple-element.28), channel_id=1, source_target_pairs={{0,4},{1,5},{2,6},{3,7},{4,0},{5,1},{6,2},{7,3},{8,12},{9,13},{10,... | collective-permute-start | bytes 589832 | tf_op jit(solution)/shard_map/ppermute | solution.py:25
  431.2 16.2 %copy-start.1 = (bf16[96,4096]{1,0:T(8,128)(2,1)S(1)}, bf16[96,4096]{1,0:T(8,128)(2,1)}, u32[]{:S(2)}) copy-start(bf16[96,4096]{1,0:T(8,128)(2,1)} %param.6) | copy-start | bytes 2359300
Sparse Core Ops, SparseCore 0:
  10.7 22.3 all-gather.6
  35.8 60.4 all-gather.10
  227.0 38.7 all-gather.8
  267.8 60.4 all-gather.12
